TPU v7x, 128 devices: a whole 4x4x4 slice. The times are simulated.
128 devices in a mesh: sub: 16 (over y, z), cont: 8 (over x, core).
Axes of the slice: x: 4, y: 4, z: 4, core: 2. Of those that a mesh axis runs over, the one named last changes fastest.
Arguments:
- schur_matrix: float32 [16, 8, 1536, 1536], P('sub', 'cont'), as said below
- load_vectors: float32 [16, 8, 1536, 512], P('sub', 'cont')
- glue_blocks: int32 [16, 8, 8], P('sub', 'cont'), may hold values from 0 to 7, each once within a row
- contact_order: int32 [16, 8, 8], P('sub', 'cont'), may hold values from 0 to 7, each once within a row
- active_flags: int32 [16, 8, 512], P('sub', 'cont'), may hold values 0 or 1
Outputs:
- glue_multipliers: float32 [16, 8, 512, 512], P('sub', 'cont')
- contact_multipliers: float32 [16, 8, 512, 512], P('sub', 'cont')
- glue_residual: float32 [16, 8, 512, 512], P('sub', 'cont')
- contact_residual: float32 [16, 8, 512, 512], P('sub', 'cont')
Inputs may be any that keep to these rules, and one draw needn't show every extreme that they name: `glue_blocks`: each row lists the 8 upper-face blocks once each. `contact_order`: each row lists the 8 contact blocks once each. `schur_matrix`: every tile is symmetric and positive definite.
All inputs are finite; a program needn't handle non-finite values. No bound on the sum of `active_flags` on one device may be relied on, other than what follows from the above.
Results may differ from a plain program's by a relative error of at most 0.0003.
Values sent between devices are 32-bit elements; how exact they have to be, the bound alone decides.
A program may use at most 128 MiB of HBM per device.

v0:
```python
import jax
import jax.numpy as jnp
from jax import lax
from jax.sharding import PartitionSpec as P

BLOCK = 64
FACE_BLOCKS = 8
CONT_BLOCKS = 8
ITERS = 2


precise = lax.Precision.HIGHEST


def from_behind(value, axis, steps):
    count = lax.axis_size(axis)
    leading, last = (max(0, -steps), min(count, count - steps))
    return lax.ppermute(value, axis, [(source, source + steps) for source in range(leading, last)])


def one_hot_rows(indices, count):
    return (indices[..., :, None] == jnp.arange(count, dtype=jnp.int32)).astype(jnp.float32)


def apply_schur(schur_tile, fields):
    return jnp.dot(schur_tile, fields, precision=precise, preferred_element_type=jnp.float32)


def jump_field(fields, glue_hot, order_hot):
    load_cols = fields.shape[1]
    blocks = fields.reshape(-1, BLOCK, load_cols)
    lower_face = blocks[:FACE_BLOCKS]
    upper_face = blocks[FACE_BLOCKS : 2 * FACE_BLOCKS]
    contact = blocks[2 * FACE_BLOCKS :]
    upper_prev = from_behind(upper_face, "sub", 1)
    glue_jump = lower_face - jnp.einsum("km,mxr->kxr", glue_hot, upper_prev, precision=precise)
    sent_blocks = jnp.einsum("pk,kxr->pxr", order_hot, contact, precision=precise)
    return (glue_jump.reshape(-1, load_cols), sent_blocks.reshape(-1, load_cols))


def spread_field(glue_vals, sent_vals, glue_hot, order_hot):
    load_cols = glue_vals.shape[1]
    lower_face = glue_vals.reshape(FACE_BLOCKS, BLOCK, load_cols)
    passed = jnp.einsum("km,kxr->mxr", glue_hot, lower_face, precision=precise)
    upper_face = -from_behind(passed, "sub", -1)
    sent_blocks = sent_vals.reshape(CONT_BLOCKS, BLOCK, load_cols)
    contact = jnp.einsum("pk,pxr->kxr", order_hot, sent_blocks, precision=precise)
    whole = jnp.concatenate([lower_face, upper_face, contact], axis=0)
    return whole.reshape(-1, load_cols)


def to_buckets(values):
    load_cols = values.shape[1]
    moved = lax.all_to_all(
        values.reshape(CONT_BLOCKS, BLOCK, load_cols),
        "cont",
        split_axis=0,
        concat_axis=0,
        tiled=True,
    )
    return moved.reshape(-1, load_cols)


def to_subdomains(values):
    load_cols = values.shape[1]
    moved = lax.all_to_all(
        values.reshape(CONT_BLOCKS, BLOCK, load_cols),
        "cont",
        split_axis=0,
        concat_axis=0,
        tiled=True,
    )
    return moved.reshape(-1, load_cols)


def column_dots(left_vec, right_vec):
    return jnp.sum(left_vec[0] * right_vec[0], axis=0) + jnp.sum(left_vec[1] * right_vec[1], axis=0)


def combine(left_vec, scaling, right_vec):
    return (left_vec[0] + scaling * right_vec[0], left_vec[1] + scaling * right_vec[1])


def global_norms(residual):
    return lax.psum(column_dots(residual, residual), ("sub", "cont"))


def global_curvature(direction, product_vec):
    return lax.psum(column_dots(direction, product_vec), ("sub", "cont"))


def per_device(schur_matrix, load_vectors, glue_blocks, contact_order, active_flags):
    schur_tile = schur_matrix[0, 0]
    load_tile = load_vectors[0, 0]
    glue_hot = one_hot_rows(glue_blocks[0, 0], FACE_BLOCKS)
    order_hot = one_hot_rows(contact_order[0, 0], CONT_BLOCKS)
    keep_mask = active_flags[0, 0].astype(jnp.float32)[:, None]
    glue_rhs, sent_rhs = jump_field(apply_schur(schur_tile, load_tile), glue_hot, order_hot)
    rhs_vec = (glue_rhs, to_buckets(sent_rhs) * keep_mask)
    residual = rhs_vec
    multipliers = (jnp.zeros_like(residual[0]), jnp.zeros_like(residual[1]))
    direction = residual
    norm_now = global_norms(residual)
    for iteration in range(ITERS):
        fields = spread_field(direction[0], to_subdomains(direction[1]), glue_hot, order_hot)
        glue_jump, sent_vals = jump_field(apply_schur(schur_tile, fields), glue_hot, order_hot)
        product_vec = (glue_jump, to_buckets(sent_vals) * keep_mask)
        step_alpha = norm_now / global_curvature(direction, product_vec)
        multipliers = combine(multipliers, step_alpha, direction)
        residual = combine(residual, -step_alpha, product_vec)
        if iteration + 1 < ITERS:
            norm_next = global_norms(residual)
            direction = combine(residual, norm_next / norm_now, direction)
            norm_now = norm_next
    contact_mult = multipliers[1]
    contact_res = residual[1]
    return (
        multipliers[0][None, None],
        contact_mult[None, None],
        residual[0][None, None],
        contact_res[None, None],
    )


def solution(mesh):
    return jax.shard_map(
        per_device,
        mesh=mesh,
        in_specs=(
            P("sub", "cont", None, None),
            P("sub", "cont", None, None),
            P("sub", "cont", None),
            P("sub", "cont", None),
            P("sub", "cont", None),
        ),
        out_specs=(
            P("sub", "cont", None, None),
            P("sub", "cont", None, None),
            P("sub", "cont", None, None),
            P("sub", "cont", None, None),
        ),
        check_vma=False,
    )
```

profile of v0, /device:TPU:1, one launch (start us, length us, event | category | flops | bytes accessed | tf_op | source)
XLA Modules:
  0.0 501.9 jit_solution(10424783602774269084)
XLA Ops:
  0.6 1.9 copy-done
  2.5 17.4 %fusion.4 = f32[1536,512]{1,0:T(8,128)S(1)} fusion(f32[1,1,1536,1536]{3,2,1,0:T(8,128)} %param.5, f32[1,1,1536,512]{3,2,1,0:T(8,128)S(1)} %copy-done), kind=kOutput, calls=%fused_computation.4 | convolution fusion | flops 14495514624 | bytes 15728640 | tf_op jit(solution)/shard_map/dot_general | solution.py:26
  19.9 1.3 fusion.53
  22.4 1.6 copy.52
  24.0 5.8 %all-to-all-start = ((f32[8,64,512]{2,1,0:T(8,128)}), f32[8,64,512]{2,1,0:T(8,128)S(1)}, u32[]{:S(2)}, u32[]{:S(2)}) async-start(f32[8,64,512]{2,1,0:T(8,128)} %copy.52), calls=%async_computation | async-start | bytes 2097152 | tf_op jit(solution)/shard_map/all_to_all | solution.py:54
  29.8 1.6 copy.49
  31.4 4.6 collective-permute-start
  36.1 8.8 %all-to-all-done = f32[8,64,512]{2,1,0:T(8,128)S(1)} async-done(((f32[8,64,512]{2,1,0:T(8,128)}), f32[8,64,512]{2,1,0:T(8,128)S(1)}, u32[]{:S(2)}, u32[]{:S(2)}) %all-to-all-start) | async-done | bytes 1048608 | tf_op jit(solution)/shard_map/all_to_all | solution.py:54
  45.5 1.6 copy.56
  47.1 4.8 all-to-all-start.1
  51.9 5.9 %collective-permute-done = f32[8,64,512]{2,0,1:T(8,128)} collective-permute-done((f32[8,64,512]{2,0,1:T(8,128)}, f32[8,64,512]{2,0,1:T(8,128)}, u32[]{:S(2)}, u32[]{:S(2)}) %collective-permute-start) | collective-permute-done | bytes 1048608 | tf_op jit(solution)/shard_map/ppermute | solution.py:18
  57.8 2.7 convolution_subtract_fusion.2
  60.5 1.7 fusion.28
  62.1 1.3 collective-permute-start.1
  63.4 3.6 all-to-all-done.1
  67.0 1.2 fusion.21
  68.3 21.0 %collective-permute-done.1 = f32[8,64,512]{2,0,1:T(8,128)} collective-permute-done((f32[8,64,512]{2,0,1:T(8,128)}, f32[8,64,512]{2,0,1:T(8,128)}, u32[]{:S(2)}, u32[]{:S(2)}) %collective-permute-start.1) | collective-permute-done | bytes 1048608 | tf_op jit(solution)/shard_map/ppermute | solution.py:18
  89.3 1.3 neg.12
  90.9 1.8 copy.59
  92.8 32.5 %fusion.6 = f32[1536,512]{0,1:T(8,128)S(1)} fusion(f32[1536,512]{1,0:T(8,128)S(1)} %bitcast.81, f32[1,1,1536,1536]{3,2,1,0:T(8,128)} %param.5), kind=kOutput, calls=%fused_computation.6 | convolution fusion | flops 14495514624 | bytes 15728640 | tf_op jit(solution)/shard_map/dot_general | solution.py:26
  125.3 1.7 fusion.52
  127.0 1.6 copy.64
  128.5 1.2 fusion.19
  129.7 1.6 copy.66
  131.3 5.4 %all-to-all-start.2 = ((f32[8,64,512]{2,1,0:T(8,128)}), f32[8,64,512]{2,1,0:T(8,128)S(1)}, u32[]{:S(2)}, u32[]{:S(2)}) async-start(f32[8,64,512]{2,1,0:T(8,128)} %copy.66), calls=%async_computation.2 | async-start | bytes 2097152 | tf_op jit(solution)/shard_map/all_to_all | solution.py:54
  136.7 2.5 copy.61
  139.2 2.8 copy.62
  142.0 4.5 collective-permute-start.2
  146.6 2.5 copy.60
  149.1 2.7 all-to-all-done.2
  151.8 1.2 multiply_reduce_fusion.3
  153.0 15.5 %collective-permute-done.2 = f32[8,64,512]{2,0,1:T(8,128)} collective-permute-done((f32[8,64,512]{2,0,1:T(8,128)}, f32[8,64,512]{2,0,1:T(8,128)}, u32[]{:S(2)}, u32[]{:S(2)}) %collective-permute-start.2) | collective-permute-done | bytes 1048608 | tf_op jit(solution)/shard_map/ppermute | solution.py:18
  168.5 3.7 multiply_reduce_fusion.4
  172.2 70.4 %all-reduce = (f32[512]{0:T(512)S(1)}, f32[512]{0:T(512)S(1)}) all-reduce(f32[512]{0:T(512)S(1)} %add.126, f32[512]{0:T(512)S(1)} %add.127), channel_id=1, replica_groups=mesh['sub'=16,'cont'=8] {'sub','cont'}, use_global_device_ids=true, to_apply=%region_2.0 | all-reduce | flops 1024 | bytes 8192 | tf_op jit(solution)/shard_map/psum | solution.py:85
  242.6 2.6 multiply_reduce_fusion.1
  245.2 63.8 %psum.30 = f32[512]{0:T(512)S(1)} all-reduce(f32[512]{0:T(512)S(1)} %add.130), channel_id=1, replica_groups=mesh['sub'=16,'cont'=8] {'sub','cont'}, use_global_device_ids=true, to_apply=%region_8.0 | all-reduce | flops 512 | bytes 4096 | tf_op jit(solution)/shard_map/psum | solution.py:85
  309.0 3.7 multiply_add_fusion.6
  313.7 1.6 copy.70
  315.3 4.4 all-to-all-start.3
  319.7 1.7 fusion.26
  321.3 1.3 collective-permute-start.3
  322.6 12.2 %all-to-all-done.3 = f32[8,64,512]{2,1,0:T(8,128)S(1)} async-done(((f32[8,64,512]{2,1,0:T(8,128)}), f32[8,64,512]{2,1,0:T(8,128)S(1)}, u32[]{:S(2)}, u32[]{:S(2)}) %all-to-all-start.3) | async-done | bytes 1048608 | tf_op jit(solution)/shard_map/all_to_all | solution.py:66
  334.8 1.2 fusion.17
  336.0 12.1 %collective-permute-done.3 = f32[8,64,512]{2,0,1:T(8,128)} collective-permute-done((f32[8,64,512]{2,0,1:T(8,128)}, f32[8,64,512]{2,0,1:T(8,128)}, u32[]{:S(2)}, u32[]{:S(2)}) %collective-permute-start.3) | collective-permute-done | bytes 1048608 | tf_op jit(solution)/shard_map/ppermute | solution.py:18
  348.2 1.3 neg.14
  349.8 1.8 copy.73
  351.6 32.3 %fusion.9 = f32[1536,512]{0,1:T(8,128)S(1)} fusion(f32[1536,512]{1,0:T(8,128)S(1)} %bitcast.82, f32[1,1,1536,1536]{3,2,1,0:T(8,128)} %param.5), kind=kOutput, calls=%fused_computation.7 | convolution fusion | flops 14495514624 | bytes 15728640 | tf_op jit(solution)/shard_map/dot_general | solution.py:26
  383.9 1.7 fusion.51
  385.6 1.6 copy.78
  387.2 1.2 fusion.15
  388.4 1.6 copy.80
  390.0 5.4 %all-to-all-start.4 = ((f32[8,64,512]{2,1,0:T(8,128)}), f32[8,64,512]{2,1,0:T(8,128)}, u32[]{:S(2)}, u32[]{:S(2)}) async-start(f32[8,64,512]{2,1,0:T(8,128)} %copy.80), calls=%async_computation.4 | async-start | bytes 2097152 | tf_op jit(solution)/shard_map/all_to_all | solution.py:54
  395.4 2.6 copy.75
  398.0 2.8 copy.76
  400.8 2.5 collective-permute-start.4
  403.4 1.6 copy.68
  405.0 1.6 copy.82
  406.5 1.6 copy.74
  408.1 2.5 all-to-all-done.4
  410.6 1.8 fusion.14
  412.5 12.8 %collective-permute-done.4 = f32[8,64,512]{2,0,1:T(8,128)} collective-permute-done((f32[8,64,512]{2,0,1:T(8,128)}, f32[8,64,512]{2,0,1:T(8,128)}, u32[]{:S(2)}, u32[]{:S(2)}) %collective-permute-start.4) | collective-permute-done | bytes 1048608 | tf_op jit(solution)/shard_map/ppermute | solution.py:18
  425.3 2.4 multiply_reduce_fusion
  427.7 68.2 %psum.31 = f32[512]{0:T(512)S(1)} all-reduce(f32[512]{0:T(512)S(1)} %add.133), channel_id=1, replica_groups=mesh['sub'=16,'cont'=8] {'sub','cont'}, use_global_device_ids=true, to_apply=%region_11.0 | all-reduce | flops 512 | bytes 4096 | tf_op jit(solution)/shard_map/psum | solution.py:89
  496.5 5.1 %multiply_add_fusion.1 = (f32[1,1,512,512]{3,2,1,0:T(8,128)}, f32[1,1,512,512]{3,2,1,0:T(8,128)}, f32[1,1,512,512]{3,2,1,0:T(8,128)}, f32[1,1,512,512]{3,2,1,0:T(8,128)}) fusion(f32[1,1,512,512]{3,2,1,0:T(8,128)S(1)} %bitcast.80, f32[1,1,512,512]{3,2,1,0:T(8,128)} %bitcast.78, f32[1,1,512,512]{3,2,1,0:T(8,128)} %bitcast.79, f32[512]{0:T(512)S(1)} %get-tuple-element.12, ...), kind=kLoop, calls=%fused_computation.30 | loop fusion | flops 5505024 | bytes 10498048 | tf_op jit(solution)/shard_map/add | solution.py:81
  (37 shorter events, 4.3 us)
Async XLA Ops:
  0.6 1.9 copy-start
  19.9 1.3 copy-start.8
  22.4 13.5 %copy-start.10 = (s32[1,1,512]{2,1,0:T(1,128)S(1)}, s32[1,1,512]{2,1,0:T(1,128)}, u32[]{:S(2)}) copy-start(s32[1,1,512]{2,1,0:T(1,128)} %param.9) | copy-start | bytes 6148
  24.0 20.9 %all-to-all-start = ((f32[8,64,512]{2,1,0:T(8,128)}), f32[8,64,512]{2,1,0:T(8,128)S(1)}, u32[]{:S(2)}, u32[]{:S(2)}) async-start(f32[8,64,512]{2,1,0:T(8,128)} %copy.52), calls=%async_computation | async-start | bytes 2097152 | tf_op jit(solution)/shard_map/all_to_all | solution.py:54
  31.4 26.4 %collective-permute-start = (f32[8,64,512]{2,0,1:T(8,128)}, f32[8,64,512]{2,0,1:T(8,128)}, u32[]{:S(2)}, u32[]{:S(2)}) collective-permute-start(f32[8,64,512]{2,0,1:T(8,128)} %copy.49), channel_id=1, source_target_pairs={{0,8},{8,16},{16,24},{24,32},{32,40},{40,48},{48,56},{56,64},{64,7... | collective-permute-start | bytes 3145736 | tf_op jit(solution)/shard_map/ppermute | solution.py:18
  36.1 21.7 %copy-start.9 = (s32[1,1,8]{2,1,0:T(1,128)S(1)}, s32[1,1,8]{2,1,0:T(1,128)}, u32[]{:S(2)}) copy-start(s32[1,1,8]{2,1,0:T(1,128)} %param.7) | copy-start | bytes 100
  44.9 264.1 %copy-start.2 = (f32[8,64,512]{2,1,0:T(8,128)}, f32[8,64,512]{2,1,0:T(8,128)S(1)}, u32[]{:S(2)}) copy-start(f32[8,64,512]{2,1,0:T(8,128)S(1)} %all-to-all-done) | copy-start | bytes 3145732
  47.1 19.9 %all-to-all-start.1 = ((f32[8,64,512]{2,1,0:T(8,128)}), f32[8,64,512]{2,1,0:T(8,128)S(1)}, u32[]{:S(2)}, u32[]{:S(2)}) async-start(f32[8,64,512]{2,1,0:T(8,128)} %copy.56), calls=%async_computation.1 | async-start | bytes 2097152 | tf_op jit(solution)/shard_map/all_to_all | solution.py:66
  62.1 27.2 %collective-permute-start.1 = (f32[8,64,512]{2,0,1:T(8,128)}, f32[8,64,512]{2,0,1:T(8,128)}, u32[]{:S(2)}, u32[]{:S(2)}) collective-permute-start(f32[8,64,512]{2,0,1:T(8,128)} %fusion.28), channel_id=1, source_target_pairs={{8,0},{16,8},{24,16},{32,24},{40,32},{48,40},{56,48},{64,56},{72,6... | collective-permute-start | bytes 3145736 | tf_op jit(solution)/shard_map/ppermute | solution.py:18
  131.3 20.5 %all-to-all-start.2 = ((f32[8,64,512]{2,1,0:T(8,128)}), f32[8,64,512]{2,1,0:T(8,128)S(1)}, u32[]{:S(2)}, u32[]{:S(2)}) async-start(f32[8,64,512]{2,1,0:T(8,128)} %copy.66), calls=%async_computation.2 | async-start | bytes 2097152 | tf_op jit(solution)/shard_map/all_to_all | solution.py:54
  142.0 26.4 %collective-permute-start.2 = (f32[8,64,512]{2,0,1:T(8,128)}, f32[8,64,512]{2,0,1:T(8,128)}, u32[]{:S(2)}, u32[]{:S(2)}) collective-permute-start(f32[8,64,512]{2,0,1:T(8,128)} %copy.62), channel_id=1, source_target_pairs={{0,8},{8,16},{16,24},{24,32},{32,40},{40,48},{48,56},{56,64},{64,7... | collective-permute-start | bytes 3145736 | tf_op jit(solution)/shard_map/ppermute | solution.py:18
  151.8 157.2 %copy-start.3 = (f32[8,64,512]{2,1,0:T(8,128)}, f32[8,64,512]{2,1,0:T(8,128)S(1)}, u32[]{:S(2)}) copy-start(f32[8,64,512]{2,1,0:T(8,128)S(1)} %all-to-all-done.2) | copy-start | bytes 3145732
  312.7 1.0 copy-start.6
  312.7 6.9 %copy-start.5 = (f32[8,64,512]{2,0,1:T(8,128)S(1)}, f32[8,64,512]{2,0,1:T(8,128)}, u32[]{:S(2)}) copy-start(f32[8,64,512]{2,0,1:T(8,128)} %get-tuple-element.32) | copy-start | bytes 3145732
  315.3 19.5 %all-to-all-start.3 = ((f32[8,64,512]{2,1,0:T(8,128)}), f32[8,64,512]{2,1,0:T(8,128)S(1)}, u32[]{:S(2)}, u32[]{:S(2)}) async-start(f32[8,64,512]{2,1,0:T(8,128)} %copy.70), calls=%async_computation.3 | async-start | bytes 2097152 | tf_op jit(solution)/shard_map/all_to_all | solution.py:66
  321.3 26.8 %collective-permute-start.3 = (f32[8,64,512]{2,0,1:T(8,128)}, f32[8,64,512]{2,0,1:T(8,128)}, u32[]{:S(2)}, u32[]{:S(2)}) collective-permute-start(f32[8,64,512]{2,0,1:T(8,128)} %fusion.26), channel_id=1, source_target_pairs={{8,0},{16,8},{24,16},{32,24},{40,32},{48,40},{56,48},{64,56},{72,6... | collective-permute-start | bytes 3145736 | tf_op jit(solution)/shard_map/ppermute | solution.py:18
  390.0 20.6 %all-to-all-start.4 = ((f32[8,64,512]{2,1,0:T(8,128)}), f32[8,64,512]{2,1,0:T(8,128)}, u32[]{:S(2)}, u32[]{:S(2)}) async-start(f32[8,64,512]{2,1,0:T(8,128)} %copy.80), calls=%async_computation.4 | async-start | bytes 2097152 | tf_op jit(solution)/shard_map/all_to_all | solution.py:54
  395.4 9.5 %copy-start.4 = (f32[8,64,512]{2,0,1:T(8,128)S(1)}, f32[8,64,512]{2,0,1:T(8,128)}, u32[]{:S(2)}) copy-start(f32[8,64,512]{2,0,1:T(8,128)} %get-tuple-element.33) | copy-start | bytes 3145732
  400.8 24.4 %collective-permute-start.4 = (f32[8,64,512]{2,0,1:T(8,128)}, f32[8,64,512]{2,0,1:T(8,128)}, u32[]{:S(2)}, u32[]{:S(2)}) collective-permute-start(f32[8,64,512]{2,0,1:T(8,128)} %copy.76), channel_id=1, source_target_pairs={{0,8},{8,16},{16,24},{24,32},{32,40},{40,48},{48,56},{56,64},{64,7... | collective-permute-start | bytes 3145736 | tf_op jit(solution)/shard_map/ppermute | solution.py:18
  405.0 5.7 %copy-start.7 = (f32[8,64,512]{2,0,1:T(8,128)S(1)}, f32[8,64,512]{2,0,1:T(8,128)}, u32[]{:S(2)}) copy-start(f32[8,64,512]{2,0,1:T(8,128)} %copy-done.6) | copy-start | bytes 3145732
  496.5 5.2 %copy-start.1 = (f32[1,1,1536,512]{3,2,1,0:T(8,128)S(1)}, f32[1,1,1536,512]{3,2,1,0:T(8,128)}, u32[]{:S(2)}) copy-start(f32[1,1,1536,512]{3,2,1,0:T(8,128)} %param.6) | copy-start | bytes 9437188
where the time goes:
time: 511 us; the launch traced here: 502 us
  blocking collectives  202 us (40%)
  matrix products  100 us (20%)
  waiting for transfers between devices  97 us (19%)
  local copies, waits for them, and re-layouts  42.7 us (8%)
  starting transfers between devices  40 us (8%)
  other arithmetic  18.4 us (4%)
    psum x2, blocking collectives, global_norms(): return lax.psum(column_dots(residual, residual), ('sub', 'cont'))  134 us
    dot_general x3, matrix products, apply_schur(): jnp.dot(schur_tile, fields, precision=precise, preferred_element_type=jnp...  82.1 us
    psum x1, blocking collectives, global_curvature(): return lax.psum(column_dots(direction, product_vec), ('sub', 'cont'))  68.2 us
    ppermute x5, waiting for transfers between devices, from_behind(): lax.ppermute(value, axis, [(source, source + steps) for source in range(l...  67.3 us
    all_to_all x3, starting transfers between devices, to_buckets(): lax.all_to_all(values.reshape(CONT_BLOCKS, BLOCK, load_cols), 'cont', spl...  16.6 us
    all_to_all x2, waiting for transfers between devices, to_subdomains(): lax.all_to_all(values.reshape(CONT_BLOCKS, BLOCK, load_cols), 'cont', spl...  15.8 us
    ppermute x5, starting transfers between devices, from_behind(): lax.ppermute(value, axis, [(source, source + steps) for source in range(l...  14.2 us
    all_to_all x3, waiting for transfers between devices, to_buckets(): lax.all_to_all(values.reshape(CONT_BLOCKS, BLOCK, load_cols), 'cont', spl...  14 us
  transfers between devices with their start and end apart: 10, of which 10 were waited for; matrix products, arithmetic and copies ran while one was open for 7% of the time, Pallas kernels for 0%

commit v1 on v0

v1 whole, which is shorter than its diff:
```python
import jax
import jax.numpy as jnp
from jax import lax
from jax.experimental import pallas as pl
from jax.experimental.pallas import tpu as pltpu
from jax.sharding import PartitionSpec as P

BLOCK = 64
NBLK = 8
FACE = BLOCK * NBLK
IFACE = 3 * FACE
LOADS = 512
CHUNKS = 2
COLS = LOADS // CHUNKS
STEPS = 3 * CHUNKS
F32 = jnp.float32
BF16 = jnp.bfloat16


def fold(x):
    return jnp.sum(x.reshape(x.shape[0] // 8, 8, COLS), axis=0)


def row_sum(x):
    return jnp.sum(x, axis=0, keepdims=True)


def kernel(
    rows, cols,
    schur, loads, glue, order, flags,
    out_gm, out_cm, out_gr, out_cr,
    stage_s, s_hi, s_lo, field, f_hi, f_lo, prod, first, mask,
    low_out, con_out, up_in_0, up_in_1, up_in_2, up_in_3, up_in_4, up_in_5, low_in, con_in, flag_in, flag_own,
    sum_own, sum_sub, part_own, sum_con, result, inverse,
    s_sem, l_sem, o_sem,
    up_ss, up_rs, low_ss, low_rs, con_ss, con_rs, flag_ss, flag_rs, sub_ss, sub_rs, cont_ss, cont_rs,
):
    up_in = (up_in_0, up_in_1, up_in_2, up_in_3, up_in_4, up_in_5)
    i = lax.axis_index("sub")
    j = lax.axis_index("cont")
    after = lax.rem(i + 1, rows)
    before = lax.rem(i + rows - 1, rows)
    has_before = i > 0
    has_after = i < rows - 1

    barrier = pltpu.get_barrier_semaphore()
    for k in range(1, rows):
        pl.semaphore_signal(barrier, 1, device_id={"sub": lax.rem(i + k, rows)})
    for k in range(1, cols):
        pl.semaphore_signal(barrier, 1, device_id={"cont": lax.rem(j + k, cols)})

    def load_copy(c):
        return pltpu.make_async_copy(loads.at[:, pl.ds(c * COLS, COLS)], field.at[c], l_sem.at[c])

    def schur_copy(r, slot):
        return pltpu.make_async_copy(schur.at[pl.ds(r, FACE)], stage_s.at[slot], s_sem.at[slot])

    load_copy(0).start()
    schur_copy(FACE, 0).start()
    schur_copy(0, 1).start()
    schur_copy(2 * FACE, 2).start()
    for c in range(1, CHUNKS):
        load_copy(c).start()

    def up_copy(s):
        return pltpu.make_async_remote_copy(
            prod.at[s, pl.ds(NBLK, NBLK)], up_in[s], up_ss.at[s], up_rs.at[s], device_id={"sub": after})

    def low_copy(s):
        return pltpu.make_async_remote_copy(
            low_out.at[s], low_in.at[s], low_ss.at[s], low_rs.at[s], device_id={"sub": before})

    def con_copy(s, k):
        t = lax.rem(j + k, cols)
        return pltpu.make_async_remote_copy(
            con_out.at[s, t], con_in.at[s, j], con_ss.at[s, k], con_rs.at[s, k], device_id={"cont": t})

    def flag_copy(k):
        return pltpu.make_async_remote_copy(
            flag_own, flag_in.at[j], flag_ss.at[k], flag_rs.at[k], device_id={"cont": lax.rem(j + k, cols)})

    def sub_copy(a, k):
        return pltpu.make_async_remote_copy(
            sum_own.at[a], sum_sub.at[a, i], sub_ss.at[a, k], sub_rs.at[a, k], device_id={"sub": lax.rem(i + k, rows)})

    def cont_copy(a, k):
        return pltpu.make_async_remote_copy(
            part_own.at[a], sum_con.at[a, j], cont_ss.at[a, k], cont_rs.at[a, k], device_id={"cont": lax.rem(j + k, cols)})

    for n, ref in enumerate((glue, order)):
        for m in range(NBLK):
            found = jnp.int32(0)
            for k in range(1, NBLK):
                found = jnp.maximum(found, k * (ref[0, k] == m).astype(jnp.int32))
            inverse[n, m] = found

    def split_store(r, x):
        hi = x.astype(BF16)
        f_hi[pl.ds(r, x.shape[0]), :] = hi
        f_lo[pl.ds(r, x.shape[0]), :] = (x - hi.astype(F32)).astype(BF16)

    def product(s, r):
        a_hi = s_hi[pl.ds(r, FACE), :]
        a_lo = s_lo[pl.ds(r, FACE), :]
        value = jnp.dot(a_hi, f_hi[...], preferred_element_type=F32)
        value = value + jnp.dot(a_hi, f_lo[...], preferred_element_type=F32)
        value = value + jnp.dot(a_lo, f_hi[...], preferred_element_type=F32)
        prod[s, pl.ds(lax.div(r, BLOCK), NBLK)] = value.reshape(NBLK, BLOCK, COLS)
        return value

    def group_row(g):
        return pl.multiple_of(jnp.where(g == 0, FACE, jnp.where(g == 1, 0, 2 * FACE)), FACE)

    def send_up(s):
        up_copy(s).start()

    def send_low(s):
        def move(m, _):
            low_out[s, m] = prod[s, inverse[0, m]]
            return 0
        lax.fori_loop(0, NBLK, move, 0)
        low_copy(s).start()

    def send_contact(s):
        def move(t, _):
            con_out[s, t] = prod[s, 2 * NBLK + order[0, t]] * mask[t]
            return 0
        lax.fori_loop(0, NBLK, move, 0)
        for k in range(1, cols):
            con_copy(s, k).start()
        con_in[s, j] = con_out[s, j]

    def glue_part(s, k):
        return prod[s, k] - jnp.where(has_before, up_in[s][glue[0, k]], 0.0)

    def upper_part(s, m):
        return jnp.where(has_after, prod[s, NBLK + m] - low_in[s, m], 0.0)

    def contact_part(s, k):
        return prod[s, 2 * NBLK + k] * mask[inverse[1, k]]

    def start_sum(a, values):
        for n, v in enumerate(values):
            sum_own[a, n] = v
            sum_sub[a, i, n] = v
        for k in range(1, rows):
            sub_copy(a, k).start()

    def pass_sum(a, count):
        for k in range(1, rows):
            sub_copy(a, k).wait_recv()
        for n in range(count):
            v = sum_sub[a, 0, n]
            for k in range(1, rows):
                v = v + sum_sub[a, k, n]
            part_own[a, n] = v
            sum_con[a, j, n] = v
        for k in range(1, cols):
            cont_copy(a, k).start()

    def end_sum(a, count):
        for k in range(1, cols):
            cont_copy(a, k).wait_recv()
        totals = []
        for n in range(count):
            v = sum_con[a, 0, n]
            for k in range(1, cols):
                v = v + sum_con[a, k, n]
            totals.append(v)
        return totals

    zero8 = jnp.zeros((8, COLS), F32)
    zero1 = jnp.zeros((1, COLS), F32)

    for c in range(CHUNKS):
        s = c
        load_copy(c).wait()

        def part(n, _):
            r = pl.multiple_of(n * 128, 128)
            split_store(r, field[c, pl.ds(r, 128), :])
            return 0
        lax.fori_loop(0, IFACE // 128, part, 0)

        def group(g, _):
            r = group_row(g)
            if c == 0:
                schur_copy(r, g).wait()
                x = stage_s[g]
                hi = x.astype(BF16)
                s_hi[pl.ds(r, FACE), :] = hi
                s_lo[pl.ds(r, FACE), :] = (x - hi.astype(F32)).astype(BF16)
            product(s, r)
            if c == 0:
                @pl.when(g == 0)
                def _():
                    pl.semaphore_wait(barrier, rows - 1 + cols - 1)
                    up_copy(0).start()

                @pl.when(g == 1)
                def _():
                    send_low(0)
            return 0
        lax.fori_loop(0, 3, group, 0)
        if c == 0:
            flag_own[...] = flags[...].astype(F32)
            for k in range(1, cols):
                flag_copy(k).start()
            flag_in[j] = flag_own[...]
        else:
            send_up(s)
            send_low(s)

    for k in range(1, cols):
        flag_copy(k).wait_recv()
    lane = lax.broadcasted_iota(jnp.int32, (BLOCK, FACE), 1)
    want = lax.broadcasted_iota(jnp.int32, (BLOCK, FACE), 0) + j * BLOCK

    def mask_of(t, _):
        picked = jnp.where(lane == want, flag_in[t], 0.0)
        mask[t] = jnp.broadcast_to(jnp.sum(picked, axis=1, keepdims=True), (BLOCK, COLS))
        return 0
    lax.fori_loop(0, NBLK, mask_of, 0)

    norms0 = []
    for c in range(CHUNKS):
        was, s = c, CHUNKS + c
        send_contact(was)
        up_copy(was).wait_recv()
        low_copy(was).wait_recv()

        def part(k, norm):
            r = pl.multiple_of(k * BLOCK, BLOCK)
            x = glue_part(was, k)
            norm = norm + fold(x * x)
            field[c, pl.ds(r, BLOCK), :] = x
            split_store(r, x)
            x = upper_part(was, k)
            field[c, pl.ds(pl.multiple_of(FACE + r, BLOCK), BLOCK), :] = x
            split_store(pl.multiple_of(FACE + r, BLOCK), x)
            x = contact_part(was, k)
            norm = norm + fold(x * x)
            field[c, pl.ds(pl.multiple_of(2 * FACE + r, BLOCK), BLOCK), :] = x
            split_store(pl.multiple_of(2 * FACE + r, BLOCK), x)
            return norm
        norm = lax.fori_loop(0, NBLK, part, zero8)

        def group(g, curv):
            r = group_row(g)
            value = product(s, r)
            return curv + fold(value * field[c, pl.ds(r, FACE), :])
        curv = lax.fori_loop(0, 3, group, zero8)
        start_sum(c, [row_sum(norm), row_sum(curv)])
        send_up(s)
        send_low(s)
        send_contact(s)
        if c > 0:
            pass_sum(c - 1, 2)

    alphas, norms, curvs, new_norms = [], [], [], []
    for c in range(CHUNKS):
        was, s = CHUNKS + c, 2 * CHUNKS + c
        up_copy(was).wait_recv()
        low_copy(was).wait_recv()
        total_norm, total_curv = end_sum(c, 2)
        alpha = total_norm / total_curv
        alphas.append(alpha)
        norms.append(total_norm)
        curvs.append(total_curv)

        def part(k, carry):
            norm, cross = carry
            r = pl.multiple_of(k * BLOCK, BLOCK)
            for n, of in enumerate((glue_part, upper_part, contact_part)):
                at = pl.multiple_of(n * FACE + r, BLOCK)
                x = field[c, pl.ds(at, BLOCK), :] - alpha * of(was, k)
                if n != 1:
                    norm = norm + fold(x * x)
                cross = cross + fold(x * prod[was, n * NBLK + k])
                first[c, pl.ds(at, BLOCK), :] = x
                split_store(at, x)
            return norm, cross
        norm, cross = lax.fori_loop(0, NBLK, part, (zero8, zero8))

        def group(g, curv):
            r = group_row(g)
            value = product(s, r)
            return curv + fold(value * first[c, pl.ds(r, FACE), :])
        curv = lax.fori_loop(0, 3, group, zero8)
        start_sum(CHUNKS + c, [row_sum(norm), row_sum(cross), row_sum(curv)])
        send_up(s)
        send_contact(s)
        if c == 0:
            pass_sum(CHUNKS - 1, 2)
        else:
            pass_sum(CHUNKS + c - 1, 3)

    for c in range(CHUNKS):
        if c == CHUNKS - 1:
            pass_sum(CHUNKS + c, 3)
        new_norm, cross, curv = end_sum(CHUNKS + c, 3)
        alpha = alphas[c]
        beta = new_norm / norms[c]
        alpha1 = new_norm / (curv + beta * (2.0 * cross + beta * curvs[c]))
        lead = alpha + alpha1 * beta
        for k in range(1, cols):
            con_copy(c, k).wait_recv()
            con_copy(CHUNKS + c, k).wait_recv()
            con_copy(2 * CHUNKS + c, k).wait_recv()

        def contact_out(k, _):
            r = pl.multiple_of(k * BLOCK, BLOCK)
            r0 = con_in[c, k]
            q0 = con_in[CHUNKS + c, k]
            r1 = r0 - alpha * q0
            result[c, 1, pl.ds(r, BLOCK), :] = lead * r0 + alpha1 * r1
            result[c, 3, pl.ds(r, BLOCK), :] = r1 - alpha1 * (con_in[2 * CHUNKS + c, k] + beta * q0)
            return 0
        lax.fori_loop(0, NBLK, contact_out, 0)

        def glue_mult(k, _):
            r = pl.multiple_of(k * BLOCK, BLOCK)
            result[c, 0, pl.ds(r, BLOCK), :] = (
                lead * field[c, pl.ds(r, BLOCK), :] + alpha1 * first[c, pl.ds(r, BLOCK), :])
            return 0
        lax.fori_loop(0, NBLK, glue_mult, 0)

        def out_copy(n, out):
            return pltpu.make_async_copy(result.at[c, n], out.at[:, pl.ds(c * COLS, COLS)], o_sem.at[c, n])
        for n, out in ((0, out_gm), (1, out_cm), (3, out_cr)):
            out_copy(n, out).start()
        up_copy(2 * CHUNKS + c).wait_recv()

        def glue_res(k, _):
            r = pl.multiple_of(k * BLOCK, BLOCK)
            x = glue_part(2 * CHUNKS + c, k) + beta * glue_part(CHUNKS + c, k)
            result[c, 2, pl.ds(r, BLOCK), :] = first[c, pl.ds(r, BLOCK), :] - alpha1 * x
            return 0
        lax.fori_loop(0, NBLK, glue_res, 0)
        out_copy(2, out_gr).start()

    for c in range(CHUNKS):
        for n, out in enumerate((out_gm, out_cm, out_gr, out_cr)):
            pltpu.make_async_copy(result.at[c, n], out.at[:, pl.ds(c * COLS, COLS)], o_sem.at[c, n]).wait()
    for s in range(STEPS):
        up_copy(s).wait_send()
        if s < 2 * CHUNKS:
            low_copy(s).wait_send()
        for k in range(1, cols):
            con_copy(s, k).wait_send()
    for k in range(1, cols):
        flag_copy(k).wait_send()
    for a in range(2 * CHUNKS):
        for k in range(1, rows):
            sub_copy(a, k).wait_send()
        for k in range(1, cols):
            cont_copy(a, k).wait_send()


def hand_on(*refs):
    ins, outs, sem = refs[:4], refs[4:8], refs[8]
    half = FACE // 2
    copies = [
        pltpu.make_async_copy(a.at[pl.ds(h * half, half)], b.at[pl.ds(h * half, half)], sem.at[n, h])
        for n, (a, b) in enumerate(zip(ins, outs)) for h in range(2)
    ]
    for copy in copies:
        copy.start()
    for copy in copies:
        copy.wait()


def per_device(schur_matrix, load_vectors, glue_blocks, contact_order, active_flags):
    rows, cols = lax.axis_size("sub"), lax.axis_size("cont")
    any_space = pl.BlockSpec(memory_space=pl.ANY)
    smem = pl.BlockSpec(memory_space=pltpu.SMEM)
    vmem = pl.BlockSpec(memory_space=pltpu.VMEM)
    dma = pltpu.SemaphoreType.DMA
    sums = 2 * CHUNKS
    outs = pl.pallas_call(
        lambda *refs: kernel(rows, cols, *refs),
        out_shape=[jax.ShapeDtypeStruct((FACE, LOADS), F32)] * 4,
        in_specs=[any_space, any_space, smem, smem, vmem],
        out_specs=[any_space] * 4,
        scratch_shapes=[
            pltpu.VMEM((3, FACE, IFACE), F32),
            pltpu.VMEM((IFACE, IFACE), BF16),
            pltpu.VMEM((IFACE, IFACE), BF16),
            pltpu.VMEM((CHUNKS, IFACE, COLS), F32),
            pltpu.VMEM((IFACE, COLS), BF16),
            pltpu.VMEM((IFACE, COLS), BF16),
            pltpu.VMEM((STEPS, 3 * NBLK, BLOCK, COLS), F32),
            pltpu.VMEM((CHUNKS, IFACE, COLS), F32),
            pltpu.VMEM((NBLK, BLOCK, COLS), F32),
            pltpu.VMEM((2 * CHUNKS, NBLK, BLOCK, COLS), F32),
            pltpu.VMEM((STEPS, NBLK, BLOCK, COLS), F32),
            *[pltpu.VMEM((NBLK, BLOCK, COLS), F32)] * STEPS,
            pltpu.VMEM((2 * CHUNKS, NBLK, BLOCK, COLS), F32),
            pltpu.VMEM((STEPS, NBLK, BLOCK, COLS), F32),
            pltpu.VMEM((cols, 1, FACE), F32),
            pltpu.VMEM((1, FACE), F32),
            pltpu.VMEM((sums, 3, 1, COLS), F32),
            pltpu.VMEM((sums, rows, 3, 1, COLS), F32),
            pltpu.VMEM((sums, 3, 1, COLS), F32),
            pltpu.VMEM((sums, cols, 3, 1, COLS), F32),
            pltpu.VMEM((CHUNKS, 4, FACE, COLS), F32),
            pltpu.SMEM((2, NBLK), jnp.int32),
            dma((3,)), dma((CHUNKS,)), dma((CHUNKS, 4)),
            dma((STEPS,)), dma((STEPS,)),
            dma((2 * CHUNKS,)), dma((2 * CHUNKS,)),
            dma((STEPS, cols)), dma((STEPS, cols)),
            dma((cols,)), dma((cols,)),
            dma((sums, rows)), dma((sums, rows)),
            dma((sums, cols)), dma((sums, cols)),
        ],
        compiler_params=pltpu.CompilerParams(
            collective_id=0, has_side_effects=True, vmem_limit_bytes=60 * 2**20),
        cost_estimate=pl.CostEstimate(
            flops=3 * 6 * IFACE * IFACE * LOADS, bytes_accessed=4 * (IFACE * IFACE + IFACE * LOADS + 4 * FACE * LOADS),
            transcendentals=0),
    )(
        schur_matrix.reshape(IFACE, IFACE),
        load_vectors.reshape(IFACE, LOADS),
        glue_blocks.reshape(1, NBLK),
        contact_order.reshape(1, NBLK),
        active_flags.reshape(1, FACE),
    )
    outs = pl.pallas_call(
        hand_on,
        out_shape=[jax.ShapeDtypeStruct((FACE, LOADS), F32)] * 4,
        in_specs=[any_space] * 4,
        out_specs=[any_space] * 4,
        scratch_shapes=[dma((4, 2))],
    )(*outs)
    return tuple(out[None, None] for out in outs)


def solution(mesh):
    return jax.shard_map(
        per_device,
        mesh=mesh,
        in_specs=(
            P("sub", "cont", None, None),
            P("sub", "cont", None, None),
            P("sub", "cont", None),
            P("sub", "cont", None),
            P("sub", "cont", None),
        ),
        out_specs=(P("sub", "cont", None, None),) * 4,
        check_vma=False,
    )
```

time: 511 us -> 217 us (0.42); the launches traced: 502 us -> 216 us
  Pallas kernels: 0 us -> 215 us
  blocking collectives: 202 us -> 0 us
  matrix products: 100 us -> 0 us
  waiting for transfers between devices: 97 us -> 0 us
  local copies, waits for them, and re-layouts: 42.7 us -> 0 us
  starting transfers between devices: 40 us -> 0 us
  other arithmetic: 18.4 us -> 0 us
    pallas_call x0 -> x2, Pallas kernels: none -> 215 us  [the longest x1 128 us: per_device(): pl.pallas_call(hand_on, out_shape=[jax.ShapeDtypeStruct((FACE, LOADS), F3...]
    psum x3 -> x0, blocking collectives: 202 us -> none  [the longest x2 134 us: global_norms(): return lax.psum(column_dots(residual, residual), ('sub', 'cont'))]
    dot_general x13 -> x0, matrix products: 100 us -> none  [the longest x3 82.1 us: apply_schur(): jnp.dot(schur_tile, fields, precision=precise, preferred_element_type=jnp...]
    ppermute x5 -> x0, waiting for transfers between devices: 67.3 us -> none  [from_behind(): lax.ppermute(value, axis, [(source, source + steps) for source in range(l...]
    all_to_all x5 -> x0, waiting for transfers between devices: 29.7 us -> none  [the longest x2 15.8 us: to_subdomains(): lax.all_to_all(values.reshape(CONT_BLOCKS, BLOCK, load_cols), 'cont', spl...]
    all_to_all x5 -> x0, starting transfers between devices: 25.8 us -> none  [the longest x3 16.6 us: to_buckets(): lax.all_to_all(values.reshape(CONT_BLOCKS, BLOCK, load_cols), 'cont', spl...]
    slice x12 -> x0, local copies, waits for them, and re-layouts: 24.3 us -> none  [the longest x5 12.3 us: jump_field(): upper_face = blocks[FACE_BLOCKS:2 * FACE_BLOCKS]]
    ppermute x5 -> x0, starting transfers between devices: 14.2 us -> none  [from_behind(): lax.ppermute(value, axis, [(source, source + steps) for source in range(l...]
  transfers between devices with their start and end apart: 10 -> 0, of which waited for: 10 -> 0; matrix products, arithmetic and copies ran while one was open for 7% -> 0% of each run, Pallas kernels for 0% -> 0%
where the time goes in v1:
time: 217 us; the launch traced here: 216 us
  Pallas kernels  215 us (99%)
    pallas_call x1, Pallas kernels, per_device(): pl.pallas_call(hand_on, out_shape=[jax.ShapeDtypeStruct((FACE, LOADS), F3...  128 us
    pallas_call x1, Pallas kernels, per_device(): pl.pallas_call(lambda *refs: kernel(rows, cols, *refs), out_shape=[jax.Sh...  87.1 us

profile of v1, /device:TPU:1, one launch (start us, length us, event | category | flops | bytes accessed | tf_op | source)
XLA Modules:
  0.0 215.9 jit_solution(14118228631653469735)
XLA Ops:
  0.6 87.1 %shard_map.84 = (f32[512,512]{1,0:T(8,128)}, f32[512,512]{1,0:T(8,128)}, f32[512,512]{1,0:T(8,128)}, f32[512,512]{1,0:T(8,128)}) custom-call(f32[1536,1536]{1,0:T(8,128)} %bitcast.9, f32[1536,512]{1,0:T(8,128)} %bitcast.10, s32[1,8]{1,0:T(1,128)} %bitcast.16, s32[1,8]{1,0:T(1,128)} %bitcast.17, s32[1,512]{1,0:T(1,128)} %bitcast.15), custom_call_target="tpu_custom_call" | custom-call | flops 21743271936 | bytes 16777216 | tf_op jit(solution)/shard_map/pallas_call | solution.py:380
  87.7 128.2 %shard_map.85 = (f32[512,512]{1,0:T(8,128)}, f32[512,512]{1,0:T(8,128)}, f32[512,512]{1,0:T(8,128)}, f32[512,512]{1,0:T(8,128)}) custom-call(f32[512,512]{1,0:T(8,128)} %get-tuple-element.12.refs_0_, f32[512,512]{1,0:T(8,128)} %get-tuple-element.13.refs_1_, f32[512,512]{1,0:T(8,128)} %get-tuple-element.14.refs_2_, f32[512,512]{1,0:T(8,128)} %get-tuple-element.15.refs_3_), custom_call_target="tpu_custom_call" | custom-call | tf_op jit(solution)/shard_map/pallas_call | solution.py:428

commit v2 on v1

--- a/solution.py
+++ b/solution.py
@@ -358,16 +358,25 @@
 
 
 def hand_on(*refs):
-    ins, outs, sem = refs[:4], refs[4:8], refs[8]
+    ins, outs, held, in_sem, out_sem = refs[:4], refs[4:8], refs[8], refs[9], refs[10]
     half = FACE // 2
-    copies = [
-        pltpu.make_async_copy(a.at[pl.ds(h * half, half)], b.at[pl.ds(h * half, half)], sem.at[n, h])
-        for n, (a, b) in enumerate(zip(ins, outs)) for h in range(2)
-    ]
-    for copy in copies:
-        copy.start()
-    for copy in copies:
-        copy.wait()
+    pieces = [(n, h) for n in range(4) for h in range(2)]
+
+    def in_copy(n, h):
+        part = pl.ds(h * half, half)
+        return pltpu.make_async_copy(ins[n].at[part], held.at[n, part], in_sem.at[n, h])
+
+    def out_copy(n, h):
+        part = pl.ds(h * half, half)
+        return pltpu.make_async_copy(held.at[n, part], outs[n].at[part], out_sem.at[n, h])
+
+    for n, h in pieces:
+        in_copy(n, h).start()
+    for n, h in pieces:
+        in_copy(n, h).wait()
+        out_copy(n, h).start()
+    for n, h in pieces:
+        out_copy(n, h).wait()
 
 
 def per_device(schur_matrix, load_vectors, glue_blocks, contact_order, active_flags):
@@ -430,7 +439,7 @@
         out_shape=[jax.ShapeDtypeStruct((FACE, LOADS), F32)] * 4,
         in_specs=[any_space] * 4,
         out_specs=[any_space] * 4,
-        scratch_shapes=[dma((4, 2))],
+        scratch_shapes=[pltpu.VMEM((4, FACE, LOADS), F32), dma((4, 2)), dma((4, 2))],
     )(*outs)
     return tuple(out[None, None] for out in outs)
 

time: 217 us -> 91.9 us (0.42)
  Pallas kernels: 215 us -> 90.6 us
    pallas_call x1, Pallas kernels: 128 us -> 3.58 us  [per_device(): pl.pallas_call(hand_on, out_shape=[jax.ShapeDtypeStruct((FACE, LOADS), F3...]
where the time goes in v2:
time: 91.9 us; the launch traced here: 91.3 us
  Pallas kernels  90.6 us (99%)
    pallas_call x1, Pallas kernels, per_device(): pl.pallas_call(lambda *refs: kernel(rows, cols, *refs), out_shape=[jax.Sh...  87.1 us
    pallas_call x1, Pallas kernels, per_device(): pl.pallas_call(hand_on, out_shape=[jax.ShapeDtypeStruct((FACE, LOADS), F3...  3.58 us

profile of v2, /device:TPU:1, one launch (start us, length us, event | category | flops | bytes accessed | tf_op | source)
XLA Modules:
  0.0 91.3 jit_solution(6487590056421422682)
XLA Ops:
  0.6 87.1 %shard_map.84 = (f32[512,512]{1,0:T(8,128)}, f32[512,512]{1,0:T(8,128)}, f32[512,512]{1,0:T(8,128)}, f32[512,512]{1,0:T(8,128)}) custom-call(f32[1536,1536]{1,0:T(8,128)} %bitcast.9, f32[1536,512]{1,0:T(8,128)} %bitcast.10, s32[1,8]{1,0:T(1,128)} %bitcast.16, s32[1,8]{1,0:T(1,128)} %bitcast.17, s32[1,512]{1,0:T(1,128)} %bitcast.15), custom_call_target="tpu_custom_call" | custom-call | flops 21743271936 | bytes 16777216 | tf_op jit(solution)/shard_map/pallas_call | solution.py:389
  87.7 3.6 %shard_map.85 = (f32[512,512]{1,0:T(8,128)}, f32[512,512]{1,0:T(8,128)}, f32[512,512]{1,0:T(8,128)}, f32[512,512]{1,0:T(8,128)}) custom-call(f32[512,512]{1,0:T(8,128)} %get-tuple-element.12.refs_0_, f32[512,512]{1,0:T(8,128)} %get-tuple-element.13.refs_1_, f32[512,512]{1,0:T(8,128)} %get-tuple-element.14.refs_2_, f32[512,512]{1,0:T(8,128)} %get-tuple-element.15.refs_3_), custom_call_target="tpu_custom_call" | custom-call | tf_op jit(solution)/shard_map/pallas_call | solution.py:437

commit v3 on v1

--- a/solution.py
+++ b/solution.py
@@ -7,11 +7,14 @@
 
 BLOCK = 64
 NBLK = 8
+HALF = NBLK // 2
 FACE = BLOCK * NBLK
 IFACE = 3 * FACE
 LOADS = 512
 CHUNKS = 2
 COLS = LOADS // CHUNKS
+PIECES = 6
+PIECE = IFACE // PIECES
 STEPS = 3 * CHUNKS
 F32 = jnp.float32
 BF16 = jnp.bfloat16
@@ -27,13 +30,13 @@
 
 def kernel(
     rows, cols,
-    schur, loads, glue, order, flags,
+    schur, loads, glue_hbm, order_hbm, flags_hbm,
     out_gm, out_cm, out_gr, out_cr,
     stage_s, s_hi, s_lo, field, f_hi, f_lo, prod, first, mask,
     low_out, con_out, up_in_0, up_in_1, up_in_2, up_in_3, up_in_4, up_in_5, low_in, con_in, flag_in, flag_own,
-    sum_own, sum_sub, part_own, sum_con, result, inverse,
-    s_sem, l_sem, o_sem,
-    up_ss, up_rs, low_ss, low_rs, con_ss, con_rs, flag_ss, flag_rs, sub_ss, sub_rs, cont_ss, cont_rs,
+    sum_own, sum_sub, part_own, sum_con, inverse, glue, order, flags,
+    s_sem, l_sem, i_sem,
+    half_ss, half_rs, up_ss, up_rs, low_ss, low_rs, con_ss, con_rs, flag_ss, flag_rs, sub_ss, sub_rs, cont_ss, cont_rs,
 ):
     up_in = (up_in_0, up_in_1, up_in_2, up_in_3, up_in_4, up_in_5)
     i = lax.axis_index("sub")
@@ -52,15 +55,27 @@
     def load_copy(c):
         return pltpu.make_async_copy(loads.at[:, pl.ds(c * COLS, COLS)], field.at[c], l_sem.at[c])
 
-    def schur_copy(r, slot):
-        return pltpu.make_async_copy(schur.at[pl.ds(r, FACE)], stage_s.at[slot], s_sem.at[slot])
-
+    def piece_row(g):
+        n = jnp.where(g == 0, 2, jnp.where(g < 3, g - 1, g))
+        return pl.multiple_of(n * PIECE, PIECE)
+
+    def schur_copy(g):
+        return pltpu.make_async_copy(schur.at[pl.ds(piece_row(g), PIECE)], stage_s.at[g], s_sem.at[g])
+
+    small_copies = [
+        pltpu.make_async_copy(a, b, i_sem.at[n])
+        for n, (a, b) in enumerate(((glue_hbm, glue), (order_hbm, order), (flags_hbm, flags)))
+    ]
     load_copy(0).start()
-    schur_copy(FACE, 0).start()
-    schur_copy(0, 1).start()
-    schur_copy(2 * FACE, 2).start()
-    for c in range(1, CHUNKS):
-        load_copy(c).start()
+    schur_copy(0).start()
+    for copy in small_copies:
+        copy.start()
+    schur_copy(1).start()
+
+    def first_up_copy(h):
+        part = pl.ds(NBLK + h * HALF, HALF)
+        return pltpu.make_async_remote_copy(
+            prod.at[0, part], up_in[0].at[pl.ds(h * HALF, HALF)], half_ss.at[h], half_rs.at[h], device_id={"sub": after})
 
     def up_copy(s):
         return pltpu.make_async_remote_copy(
@@ -79,33 +94,37 @@
         return pltpu.make_async_remote_copy(
             flag_own, flag_in.at[j], flag_ss.at[k], flag_rs.at[k], device_id={"cont": lax.rem(j + k, cols)})
 
+    def held(a):
+        return pl.ds(0, 2 if a < CHUNKS else 3)
+
     def sub_copy(a, k):
         return pltpu.make_async_remote_copy(
-            sum_own.at[a], sum_sub.at[a, i], sub_ss.at[a, k], sub_rs.at[a, k], device_id={"sub": lax.rem(i + k, rows)})
+            sum_own.at[a, held(a)], sum_sub.at[a, i, held(a)], sub_ss.at[a, k], sub_rs.at[a, k], device_id={"sub": lax.rem(i + k, rows)})
 
     def cont_copy(a, k):
         return pltpu.make_async_remote_copy(
-            part_own.at[a], sum_con.at[a, j], cont_ss.at[a, k], cont_rs.at[a, k], device_id={"cont": lax.rem(j + k, cols)})
-
-    for n, ref in enumerate((glue, order)):
-        for m in range(NBLK):
-            found = jnp.int32(0)
-            for k in range(1, NBLK):
-                found = jnp.maximum(found, k * (ref[0, k] == m).astype(jnp.int32))
-            inverse[n, m] = found
+            part_own.at[a, held(a)], sum_con.at[a, j, held(a)], cont_ss.at[a, k], cont_rs.at[a, k], device_id={"cont": lax.rem(j + k, cols)})
+
+    def make_inverse():
+        for n, ref in enumerate((glue, order)):
+            for m in range(NBLK):
+                found = jnp.int32(0)
+                for k in range(1, NBLK):
+                    found = jnp.maximum(found, k * (ref[0, k] == m).astype(jnp.int32))
+                inverse[n, m] = found
 
     def split_store(r, x):
         hi = x.astype(BF16)
         f_hi[pl.ds(r, x.shape[0]), :] = hi
         f_lo[pl.ds(r, x.shape[0]), :] = (x - hi.astype(F32)).astype(BF16)
 
-    def product(s, r):
-        a_hi = s_hi[pl.ds(r, FACE), :]
-        a_lo = s_lo[pl.ds(r, FACE), :]
+    def product(s, r, size=FACE):
+        a_hi = s_hi[pl.ds(r, size), :]
+        a_lo = s_lo[pl.ds(r, size), :]
         value = jnp.dot(a_hi, f_hi[...], preferred_element_type=F32)
         value = value + jnp.dot(a_hi, f_lo[...], preferred_element_type=F32)
         value = value + jnp.dot(a_lo, f_hi[...], preferred_element_type=F32)
-        prod[s, pl.ds(lax.div(r, BLOCK), NBLK)] = value.reshape(NBLK, BLOCK, COLS)
+        prod[s, pl.ds(lax.div(r, BLOCK), size // BLOCK)] = value.reshape(size // BLOCK, BLOCK, COLS)
         return value
 
     def group_row(g):
@@ -172,44 +191,64 @@
     zero8 = jnp.zeros((8, COLS), F32)
     zero1 = jnp.zeros((1, COLS), F32)
 
-    for c in range(CHUNKS):
-        s = c
-        load_copy(c).wait()
-
+    def split_loads(c):
         def part(n, _):
             r = pl.multiple_of(n * 128, 128)
             split_store(r, field[c, pl.ds(r, 128), :])
             return 0
         lax.fori_loop(0, IFACE // 128, part, 0)
 
+    load_copy(0).wait()
+    schur_copy(2).start()
+    split_loads(0)
+
+    def piece(g, _):
+        r = piece_row(g)
+        schur_copy(g).wait()
+
+        @pl.when(g < PIECES - 3)
+        def _():
+            schur_copy(g + 3).start()
+        x = stage_s[g]
+        hi = x.astype(BF16)
+        s_hi[pl.ds(r, PIECE), :] = hi
+        s_lo[pl.ds(r, PIECE), :] = (x - hi.astype(F32)).astype(BF16)
+        product(0, r, PIECE)
+
+        @pl.when(g == 0)
+        def _():
+            pl.semaphore_wait(barrier, rows - 1 + cols - 1)
+            first_up_copy(0).start()
+            for copy in small_copies:
+                copy.wait()
+            make_inverse()
+
+        @pl.when(g == 2)
+        def _():
+            send_low(0)
+
+        @pl.when(g == 3)
+        def _():
+            first_up_copy(1).start()
+            for c in range(1, CHUNKS):
+                load_copy(c).start()
+        return 0
+    lax.fori_loop(0, PIECES, piece, 0)
+    flag_own[...] = flags[...].astype(F32)
+    for k in range(1, cols):
+        flag_copy(k).start()
+    flag_in[j] = flag_own[...]
+
+    for c in range(1, CHUNKS):
+        load_copy(c).wait()
+        split_loads(c)
+
         def group(g, _):
-            r = group_row(g)
-            if c == 0:
-                schur_copy(r, g).wait()
-                x = stage_s[g]
-                hi = x.astype(BF16)
-                s_hi[pl.ds(r, FACE), :] = hi
-                s_lo[pl.ds(r, FACE), :] = (x - hi.astype(F32)).astype(BF16)
-            product(s, r)
-            if c == 0:
-                @pl.when(g == 0)
-                def _():
-                    pl.semaphore_wait(barrier, rows - 1 + cols - 1)
-                    up_copy(0).start()
-
-                @pl.when(g == 1)
-                def _():
-                    send_low(0)
+            product(c, group_row(g))
             return 0
         lax.fori_loop(0, 3, group, 0)
-        if c == 0:
-            flag_own[...] = flags[...].astype(F32)
-            for k in range(1, cols):
-                flag_copy(k).start()
-            flag_in[j] = flag_own[...]
-        else:
-            send_up(s)
-            send_low(s)
+        send_up(c)
+        send_low(c)
 
     for k in range(1, cols):
         flag_copy(k).wait_recv()
@@ -226,7 +265,11 @@
     for c in range(CHUNKS):
         was, s = c, CHUNKS + c
         send_contact(was)
-        up_copy(was).wait_recv()
+        if c == 0:
+            first_up_copy(0).wait_recv()
+            first_up_copy(1).wait_recv()
+        else:
+            up_copy(was).wait_recv()
         low_copy(was).wait_recv()
 
         def part(k, norm):
@@ -313,41 +356,36 @@
             r0 = con_in[c, k]
             q0 = con_in[CHUNKS + c, k]
             r1 = r0 - alpha * q0
-            result[c, 1, pl.ds(r, BLOCK), :] = lead * r0 + alpha1 * r1
-            result[c, 3, pl.ds(r, BLOCK), :] = r1 - alpha1 * (con_in[2 * CHUNKS + c, k] + beta * q0)
+            out_cm[pl.ds(r, BLOCK), pl.ds(c * COLS, COLS)] = lead * r0 + alpha1 * r1
+            out_cr[pl.ds(r, BLOCK), pl.ds(c * COLS, COLS)] = r1 - alpha1 * (con_in[2 * CHUNKS + c, k] + beta * q0)
             return 0
         lax.fori_loop(0, NBLK, contact_out, 0)
 
         def glue_mult(k, _):
             r = pl.multiple_of(k * BLOCK, BLOCK)
-            result[c, 0, pl.ds(r, BLOCK), :] = (
+            out_gm[pl.ds(r, BLOCK), pl.ds(c * COLS, COLS)] = (
                 lead * field[c, pl.ds(r, BLOCK), :] + alpha1 * first[c, pl.ds(r, BLOCK), :])
             return 0
         lax.fori_loop(0, NBLK, glue_mult, 0)
 
-        def out_copy(n, out):
-            return pltpu.make_async_copy(result.at[c, n], out.at[:, pl.ds(c * COLS, COLS)], o_sem.at[c, n])
-        for n, out in ((0, out_gm), (1, out_cm), (3, out_cr)):
-            out_copy(n, out).start()
         up_copy(2 * CHUNKS + c).wait_recv()
 
         def glue_res(k, _):
             r = pl.multiple_of(k * BLOCK, BLOCK)
             x = glue_part(2 * CHUNKS + c, k) + beta * glue_part(CHUNKS + c, k)
-            result[c, 2, pl.ds(r, BLOCK), :] = first[c, pl.ds(r, BLOCK), :] - alpha1 * x
+            out_gr[pl.ds(r, BLOCK), pl.ds(c * COLS, COLS)] = first[c, pl.ds(r, BLOCK), :] - alpha1 * x
             return 0
         lax.fori_loop(0, NBLK, glue_res, 0)
-        out_copy(2, out_gr).start()
-
-    for c in range(CHUNKS):
-        for n, out in enumerate((out_gm, out_cm, out_gr, out_cr)):
-            pltpu.make_async_copy(result.at[c, n], out.at[:, pl.ds(c * COLS, COLS)], o_sem.at[c, n]).wait()
+
     for s in range(STEPS):
-        up_copy(s).wait_send()
+        if s > 0:
+            up_copy(s).wait_send()
         if s < 2 * CHUNKS:
             low_copy(s).wait_send()
         for k in range(1, cols):
             con_copy(s, k).wait_send()
+    first_up_copy(0).wait_send()
+    first_up_copy(1).wait_send()
     for k in range(1, cols):
         flag_copy(k).wait_send()
     for a in range(2 * CHUNKS):
@@ -359,11 +397,7 @@
 
 def hand_on(*refs):
     ins, outs, sem = refs[:4], refs[4:8], refs[8]
-    half = FACE // 2
-    copies = [
-        pltpu.make_async_copy(a.at[pl.ds(h * half, half)], b.at[pl.ds(h * half, half)], sem.at[n, h])
-        for n, (a, b) in enumerate(zip(ins, outs)) for h in range(2)
-    ]
+    copies = [pltpu.make_async_copy(a, b, sem.at[n]) for n, (a, b) in enumerate(zip(ins, outs))]
     for copy in copies:
         copy.start()
     for copy in copies:
@@ -373,17 +407,16 @@
 def per_device(schur_matrix, load_vectors, glue_blocks, contact_order, active_flags):
     rows, cols = lax.axis_size("sub"), lax.axis_size("cont")
     any_space = pl.BlockSpec(memory_space=pl.ANY)
-    smem = pl.BlockSpec(memory_space=pltpu.SMEM)
     vmem = pl.BlockSpec(memory_space=pltpu.VMEM)
     dma = pltpu.SemaphoreType.DMA
     sums = 2 * CHUNKS
     outs = pl.pallas_call(
         lambda *refs: kernel(rows, cols, *refs),
-        out_shape=[jax.ShapeDtypeStruct((FACE, LOADS), F32)] * 4,
-        in_specs=[any_space, any_space, smem, smem, vmem],
-        out_specs=[any_space] * 4,
+        out_shape=[pltpu.VMEM((FACE, LOADS), F32)] * 4,
+        in_specs=[any_space] * 5,
+        out_specs=[vmem] * 4,
         scratch_shapes=[
-            pltpu.VMEM((3, FACE, IFACE), F32),
+            pltpu.VMEM((PIECES, PIECE, IFACE), F32),
             pltpu.VMEM((IFACE, IFACE), BF16),
             pltpu.VMEM((IFACE, IFACE), BF16),
             pltpu.VMEM((CHUNKS, IFACE, COLS), F32),
@@ -403,10 +436,12 @@
             pltpu.VMEM((sums, rows, 3, 1, COLS), F32),
             pltpu.VMEM((sums, 3, 1, COLS), F32),
             pltpu.VMEM((sums, cols, 3, 1, COLS), F32),
-            pltpu.VMEM((CHUNKS, 4, FACE, COLS), F32),
             pltpu.SMEM((2, NBLK), jnp.int32),
-            dma((3,)), dma((CHUNKS,)), dma((CHUNKS, 4)),
-            dma((STEPS,)), dma((STEPS,)),
+            pltpu.SMEM((1, NBLK), jnp.int32),
+            pltpu.SMEM((1, NBLK), jnp.int32),
+            pltpu.VMEM((1, FACE), jnp.int32),
+            dma((PIECES,)), dma((CHUNKS,)), dma((3,)),
+            dma((2,)), dma((2,)), dma((STEPS,)), dma((STEPS,)),
             dma((2 * CHUNKS,)), dma((2 * CHUNKS,)),
             dma((STEPS, cols)), dma((STEPS, cols)),
             dma((cols,)), dma((cols,)),
@@ -414,7 +449,7 @@
             dma((sums, cols)), dma((sums, cols)),
         ],
         compiler_params=pltpu.CompilerParams(
-            collective_id=0, has_side_effects=True, vmem_limit_bytes=60 * 2**20),
+            collective_id=0, has_side_effects=True, vmem_limit_bytes=54 * 2**20),
         cost_estimate=pl.CostEstimate(
             flops=3 * 6 * IFACE * IFACE * LOADS, bytes_accessed=4 * (IFACE * IFACE + IFACE * LOADS + 4 * FACE * LOADS),
             transcendentals=0),
@@ -428,9 +463,10 @@
     outs = pl.pallas_call(
         hand_on,
         out_shape=[jax.ShapeDtypeStruct((FACE, LOADS), F32)] * 4,
-        in_specs=[any_space] * 4,
+        in_specs=[vmem] * 4,
         out_specs=[any_space] * 4,
-        scratch_shapes=[dma((4, 2))],
+        scratch_shapes=[dma((4,))],
+        compiler_params=pltpu.CompilerParams(vmem_limit_bytes=4 * 2**20),
     )(*outs)
     return tuple(out[None, None] for out in outs)
 

time: 217 us -> 89.3 us (0.41)
  Pallas kernels: 215 us -> 87.3 us
    pallas_call x1, Pallas kernels: 128 us -> 2.04 us  [per_device(): pl.pallas_call(hand_on, out_shape=[jax.ShapeDtypeStruct((FACE, LOADS), F3...]
where the time goes in v3:
time: 89.3 us; the launch traced here: 87.9 us
  Pallas kernels  87.3 us (98%)
    pallas_call x1, Pallas kernels, per_device(): pl.pallas_call(lambda *refs: kernel(rows, cols, *refs), out_shape=[pltpu....  85.2 us
    pallas_call x1, Pallas kernels, per_device(): pl.pallas_call(hand_on, out_shape=[jax.ShapeDtypeStruct((FACE, LOADS), F3...  2.04 us

profile of v3, /device:TPU:1, one launch (start us, length us, event | category | flops | bytes accessed | tf_op | source)
XLA Modules:
  0.0 87.9 jit_solution(12507535795302046035)
XLA Ops:
  0.6 85.2 %shard_map.84 = (f32[512,512]{1,0:T(8,128)S(1)}, f32[512,512]{1,0:T(8,128)S(1)}, f32[512,512]{1,0:T(8,128)S(1)}, f32[512,512]{1,0:T(8,128)S(1)}) custom-call(f32[1536,1536]{1,0:T(8,128)} %bitcast.9, f32[1536,512]{1,0:T(8,128)} %bitcast.10, s32[1,8]{1,0:T(1,128)} %bitcast.16, s32[1,8]{1,0:T(1,128)} %bitcast.17, s32[1,512]{1,0:T(1,128)} %bitcast.15), custom_call_target="tpu_custom_call" | custom-call | flops 21743271936 | bytes 16777216 | tf_op jit(solution)/shard_map/pallas_call | solution.py:413
  85.9 2.0 %shard_map.85 = (f32[512,512]{1,0:T(8,128)}, f32[512,512]{1,0:T(8,128)}, f32[512,512]{1,0:T(8,128)}, f32[512,512]{1,0:T(8,128)}) custom-call(f32[512,512]{1,0:T(8,128)S(1)} %get-tuple-element.12.refs_0_, f32[512,512]{1,0:T(8,128)S(1)} %get-tuple-element.13.refs_1_, f32[512,512]{1,0:T(8,128)S(1)} %get-tuple-element.14.refs_2_, ...), custom_call_target="tpu_custom_call" | custom-call | tf_op jit(solution)/shard_map/pallas_call | solution.py:463

commit v4 on v3

--- a/solution.py
+++ b/solution.py
@@ -8,6 +8,8 @@
 BLOCK = 64
 NBLK = 8
 HALF = NBLK // 2
+ROUND = 3
+RING = 4
 FACE = BLOCK * NBLK
 IFACE = 3 * FACE
 LOADS = 512
@@ -34,9 +36,9 @@
     out_gm, out_cm, out_gr, out_cr,
     stage_s, s_hi, s_lo, field, f_hi, f_lo, prod, first, mask,
     low_out, con_out, up_in_0, up_in_1, up_in_2, up_in_3, up_in_4, up_in_5, low_in, con_in, flag_in, flag_own,
-    sum_own, sum_sub, part_own, sum_con, inverse, glue, order, flags,
+    sum_own, sum_sub, part_own, sum_con, inverse, glue, order, flags, relay_1, relay_2,
     s_sem, l_sem, i_sem,
-    half_ss, half_rs, up_ss, up_rs, low_ss, low_rs, con_ss, con_rs, flag_ss, flag_rs, sub_ss, sub_rs, cont_ss, cont_rs,
+    last_ss, last_rs, hop_ss, hop_rs, half_ss, half_rs, up_ss, up_rs, low_ss, low_rs, con_ss, con_rs, flag_ss, flag_rs, sub_ss, sub_rs, cont_ss, cont_rs,
 ):
     up_in = (up_in_0, up_in_1, up_in_2, up_in_3, up_in_4, up_in_5)
     i = lax.axis_index("sub")
@@ -77,9 +79,29 @@
         return pltpu.make_async_remote_copy(
             prod.at[0, part], up_in[0].at[pl.ds(h * HALF, HALF)], half_ss.at[h], half_rs.at[h], device_id={"sub": after})
 
+    def last_up_copy(h):
+        s = STEPS - 1
+        return pltpu.make_async_remote_copy(
+            prod.at[s, pl.ds(NBLK + h * HALF, HALF)], up_in[s].at[pl.ds(h * HALF, HALF)], last_ss.at[h], last_rs.at[h],
+            device_id={"sub": after})
+
     def up_copy(s):
-        return pltpu.make_async_remote_copy(
-            prod.at[s, pl.ds(NBLK, NBLK)], up_in[s], up_ss.at[s], up_rs.at[s], device_id={"sub": after})
+        count = NBLK - ROUND if s == 2 * CHUNKS else NBLK
+        return pltpu.make_async_remote_copy(
+            prod.at[s, pl.ds(NBLK, count)], up_in[s].at[pl.ds(0, count)], up_ss.at[s], up_rs.at[s],
+            device_id={"sub": after})
+
+    ring = lax.rem(i, RING)
+    ring_down = i - ring + lax.rem(ring + RING - 1, RING)
+    two_down_after = lax.rem(i - ring + lax.rem(ring + 2, RING) + 1, rows)
+
+    def hop_copy(n):
+        s = 2 * CHUNKS
+        kept = pl.ds(NBLK - ROUND, ROUND)
+        src = (prod.at[s, pl.ds(2 * NBLK - ROUND, ROUND)], relay_1, relay_2)[n]
+        dst = (relay_1, relay_2, up_in[s].at[kept])[n]
+        to = (ring_down, ring_down, two_down_after)[n]
+        return pltpu.make_async_remote_copy(src, dst, hop_ss.at[n], hop_rs.at[n], device_id={"sub": to})
 
     def low_copy(s):
         return pltpu.make_async_remote_copy(
@@ -129,6 +151,9 @@
 
     def group_row(g):
         return pl.multiple_of(jnp.where(g == 0, FACE, jnp.where(g == 1, 0, 2 * FACE)), FACE)
+
+    def product_row(g):
+        return pl.multiple_of((2 - g) * FACE, FACE)
 
     def send_up(s):
         up_copy(s).start()
@@ -261,10 +286,11 @@
         return 0
     lax.fori_loop(0, NBLK, mask_of, 0)
 
-    norms0 = []
+    for c in range(CHUNKS):
+        send_contact(c)
+
     for c in range(CHUNKS):
         was, s = c, CHUNKS + c
-        send_contact(was)
         if c == 0:
             first_up_copy(0).wait_recv()
             first_up_copy(1).wait_recv()
@@ -288,19 +314,23 @@
             return norm
         norm = lax.fori_loop(0, NBLK, part, zero8)
 
+        if c > 0:
+            pass_sum(c - 1, 2)
+
         def group(g, curv):
-            r = group_row(g)
+            r = product_row(g)
             value = product(s, r)
+
+            @pl.when(g == 0)
+            def _():
+                send_contact(s)
             return curv + fold(value * field[c, pl.ds(r, FACE), :])
         curv = lax.fori_loop(0, 3, group, zero8)
         start_sum(c, [row_sum(norm), row_sum(curv)])
         send_up(s)
         send_low(s)
-        send_contact(s)
-        if c > 0:
-            pass_sum(c - 1, 2)
-
-    alphas, norms, curvs, new_norms = [], [], [], []
+
+    alphas, norms, curvs = [], [], []
     for c in range(CHUNKS):
         was, s = CHUNKS + c, 2 * CHUNKS + c
         up_copy(was).wait_recv()
@@ -325,19 +355,34 @@
             return norm, cross
         norm, cross = lax.fori_loop(0, NBLK, part, (zero8, zero8))
 
-        def group(g, curv):
-            r = group_row(g)
-            value = product(s, r)
-            return curv + fold(value * first[c, pl.ds(r, FACE), :])
-        curv = lax.fori_loop(0, 3, group, zero8)
-        start_sum(CHUNKS + c, [row_sum(norm), row_sum(cross), row_sum(curv)])
-        send_up(s)
-        send_contact(s)
         if c == 0:
             pass_sum(CHUNKS - 1, 2)
         else:
             pass_sum(CHUNKS + c - 1, 3)
 
+        def group(g, curv):
+            r = product_row(g)
+            value = product(s, r)
+
+            @pl.when(g == 0)
+            def _():
+                send_contact(s)
+            if c > 0:
+                @pl.when(g == 1)
+                def _():
+                    last_up_copy(0).start()
+            return curv + fold(value * first[c, pl.ds(r, FACE), :])
+        curv = lax.fori_loop(0, 3, group, zero8)
+        start_sum(CHUNKS + c, [row_sum(norm), row_sum(cross), row_sum(curv)])
+        if c == 0:
+            send_up(s)
+            hop_copy(0).start()
+        else:
+            last_up_copy(1).start()
+            hop_copy(0).wait_recv()
+            hop_copy(1).start()
+
+    scales = []
     for c in range(CHUNKS):
         if c == CHUNKS - 1:
             pass_sum(CHUNKS + c, 3)
@@ -368,7 +413,20 @@
             return 0
         lax.fori_loop(0, NBLK, glue_mult, 0)
 
-        up_copy(2 * CHUNKS + c).wait_recv()
+        if c == 0:
+            hop_copy(1).wait_recv()
+            hop_copy(2).start()
+
+        scales.append((alpha1, beta))
+
+    for c in range(CHUNKS):
+        alpha1, beta = scales[c]
+        if c == 0:
+            up_copy(2 * CHUNKS).wait_recv()
+            hop_copy(2).wait_recv()
+        else:
+            last_up_copy(0).wait_recv()
+            last_up_copy(1).wait_recv()
 
         def glue_res(k, _):
             r = pl.multiple_of(k * BLOCK, BLOCK)
@@ -378,14 +436,17 @@
         lax.fori_loop(0, NBLK, glue_res, 0)
 
     for s in range(STEPS):
-        if s > 0:
+        if 0 < s < STEPS - 1:
             up_copy(s).wait_send()
         if s < 2 * CHUNKS:
             low_copy(s).wait_send()
         for k in range(1, cols):
             con_copy(s, k).wait_send()
-    first_up_copy(0).wait_send()
-    first_up_copy(1).wait_send()
+    for n in range(3):
+        hop_copy(n).wait_send()
+    for h in range(2):
+        first_up_copy(h).wait_send()
+        last_up_copy(h).wait_send()
     for k in range(1, cols):
         flag_copy(k).wait_send()
     for a in range(2 * CHUNKS):
@@ -440,8 +501,10 @@
             pltpu.SMEM((1, NBLK), jnp.int32),
             pltpu.SMEM((1, NBLK), jnp.int32),
             pltpu.VMEM((1, FACE), jnp.int32),
+            pltpu.VMEM((ROUND, BLOCK, COLS), F32),
+            pltpu.VMEM((ROUND, BLOCK, COLS), F32),
             dma((PIECES,)), dma((CHUNKS,)), dma((3,)),
-            dma((2,)), dma((2,)), dma((STEPS,)), dma((STEPS,)),
+            dma((2,)), dma((2,)), dma((3,)), dma((3,)), dma((2,)), dma((2,)), dma((STEPS,)), dma((STEPS,)),
             dma((2 * CHUNKS,)), dma((2 * CHUNKS,)),
             dma((STEPS, cols)), dma((STEPS, cols)),
             dma((cols,)), dma((cols,)),

time: 89.3 us -> 84.9 us (0.951); the launches traced: 87.9 us -> 84.8 us
  Pallas kernels: 87.3 us -> 84.1 us
    pallas_call x1, Pallas kernels: 85.2 us -> 82.1 us  [per_device(): pl.pallas_call(lambda *refs: kernel(rows, cols, *refs), out_shape=[pltpu....]
where the time goes in v4:
time: 84.9 us; the launch traced here: 84.8 us
  Pallas kernels  84.1 us (99%)
    pallas_call x1, Pallas kernels, per_device(): pl.pallas_call(lambda *refs: kernel(rows, cols, *refs), out_shape=[pltpu....  82.1 us
    pallas_call x1, Pallas kernels, per_device(): pl.pallas_call(hand_on, out_shape=[jax.ShapeDtypeStruct((FACE, LOADS), F3...  2.04 us

profile of v4, /device:TPU:1, one launch (start us, length us, event | category | flops | bytes accessed | tf_op | source)
XLA Modules:
  0.0 84.8 jit_solution(1768958720006215075)
XLA Ops:
  0.6 82.1 %shard_map.84 = (f32[512,512]{1,0:T(8,128)S(1)}, f32[512,512]{1,0:T(8,128)S(1)}, f32[512,512]{1,0:T(8,128)S(1)}, f32[512,512]{1,0:T(8,128)S(1)}) custom-call(f32[1536,1536]{1,0:T(8,128)} %bitcast.9, f32[1536,512]{1,0:T(8,128)} %bitcast.10, s32[1,8]{1,0:T(1,128)} %bitcast.16, s32[1,8]{1,0:T(1,128)} %bitcast.17, s32[1,512]{1,0:T(1,128)} %bitcast.15), custom_call_target="tpu_custom_call" | custom-call | flops 21743271936 | bytes 16777216 | tf_op jit(solution)/shard_map/pallas_call | solution.py:474
  82.7 2.0 %shard_map.85 = (f32[512,512]{1,0:T(8,128)}, f32[512,512]{1,0:T(8,128)}, f32[512,512]{1,0:T(8,128)}, f32[512,512]{1,0:T(8,128)}) custom-call(f32[512,512]{1,0:T(8,128)S(1)} %get-tuple-element.12.refs_0_, f32[512,512]{1,0:T(8,128)S(1)} %get-tuple-element.13.refs_1_, f32[512,512]{1,0:T(8,128)S(1)} %get-tuple-element.14.refs_2_, ...), custom_call_target="tpu_custom_call" | custom-call | tf_op jit(solution)/shard_map/pallas_call | solution.py:526

commit v5 on v4

--- a/solution.py
+++ b/solution.py
@@ -10,6 +10,7 @@
 HALF = NBLK // 2
 ROUND = 3
 RING = 4
+EARLY = 2
 FACE = BLOCK * NBLK
 IFACE = 3 * FACE
 LOADS = 512
@@ -81,8 +82,9 @@
 
     def last_up_copy(h):
         s = STEPS - 1
-        return pltpu.make_async_remote_copy(
-            prod.at[s, pl.ds(NBLK + h * HALF, HALF)], up_in[s].at[pl.ds(h * HALF, HALF)], last_ss.at[h], last_rs.at[h],
+        count = NBLK - EARLY if h else EARLY
+        return pltpu.make_async_remote_copy(
+            prod.at[s, pl.ds(NBLK + h * EARLY, count)], up_in[s].at[pl.ds(h * EARLY, count)], last_ss.at[h], last_rs.at[h],
             device_id={"sub": after})
 
     def up_copy(s):
@@ -384,8 +386,6 @@
 
     scales = []
     for c in range(CHUNKS):
-        if c == CHUNKS - 1:
-            pass_sum(CHUNKS + c, 3)
         new_norm, cross, curv = end_sum(CHUNKS + c, 3)
         alpha = alphas[c]
         beta = new_norm / norms[c]
@@ -414,6 +414,7 @@
         lax.fori_loop(0, NBLK, glue_mult, 0)
 
         if c == 0:
+            pass_sum(STEPS - CHUNKS - 1, 3)
             hop_copy(1).wait_recv()
             hop_copy(2).start()
 

time: 84.9 us -> 82.3 us (0.969)
  Pallas kernels: 84.1 us -> 81.2 us
    pallas_call x1, Pallas kernels: 82.1 us -> 79.1 us  [per_device(): pl.pallas_call(lambda *refs: kernel(rows, cols, *refs), out_shape=[pltpu....]
where the time goes in v5:
time: 82.3 us; the launch traced here: 81.8 us
  Pallas kernels  81.2 us (99%)
    pallas_call x1, Pallas kernels, per_device(): pl.pallas_call(lambda *refs: kernel(rows, cols, *refs), out_shape=[pltpu....  79.1 us
    pallas_call x1, Pallas kernels, per_device(): pl.pallas_call(hand_on, out_shape=[jax.ShapeDtypeStruct((FACE, LOADS), F3...  2.04 us

profile of v5, /device:TPU:1, one launch (start us, length us, event | category | flops | bytes accessed | tf_op | source)
XLA Modules:
  0.0 81.8 jit_solution(12831407643376266306)
XLA Ops:
  0.6 79.1 %shard_map.84 = (f32[512,512]{1,0:T(8,128)S(1)}, f32[512,512]{1,0:T(8,128)S(1)}, f32[512,512]{1,0:T(8,128)S(1)}, f32[512,512]{1,0:T(8,128)S(1)}) custom-call(f32[1536,1536]{1,0:T(8,128)} %bitcast.9, f32[1536,512]{1,0:T(8,128)} %bitcast.10, s32[1,8]{1,0:T(1,128)} %bitcast.16, s32[1,8]{1,0:T(1,128)} %bitcast.17, s32[1,512]{1,0:T(1,128)} %bitcast.15), custom_call_target="tpu_custom_call" | custom-call | flops 21743271936 | bytes 16777216 | tf_op jit(solution)/shard_map/pallas_call | solution.py:475
  79.8 2.0 %shard_map.85 = (f32[512,512]{1,0:T(8,128)}, f32[512,512]{1,0:T(8,128)}, f32[512,512]{1,0:T(8,128)}, f32[512,512]{1,0:T(8,128)}) custom-call(f32[512,512]{1,0:T(8,128)S(1)} %get-tuple-element.12.refs_0_, f32[512,512]{1,0:T(8,128)S(1)} %get-tuple-element.13.refs_1_, f32[512,512]{1,0:T(8,128)S(1)} %get-tuple-element.14.refs_2_, ...), custom_call_target="tpu_custom_call" | custom-call | tf_op jit(solution)/shard_map/pallas_call | solution.py:527

commit v6 on v5

--- a/solution.py
+++ b/solution.py
@@ -49,12 +49,6 @@
     has_before = i > 0
     has_after = i < rows - 1
 
-    barrier = pltpu.get_barrier_semaphore()
-    for k in range(1, rows):
-        pl.semaphore_signal(barrier, 1, device_id={"sub": lax.rem(i + k, rows)})
-    for k in range(1, cols):
-        pl.semaphore_signal(barrier, 1, device_id={"cont": lax.rem(j + k, cols)})
-
     def load_copy(c):
         return pltpu.make_async_copy(loads.at[:, pl.ds(c * COLS, COLS)], field.at[c], l_sem.at[c])
 
@@ -74,6 +68,12 @@
     for copy in small_copies:
         copy.start()
     schur_copy(1).start()
+
+    barrier = pltpu.get_barrier_semaphore()
+    for k in range(1, rows):
+        pl.semaphore_signal(barrier, 1, device_id={"sub": lax.rem(i + k, rows)})
+    for k in range(1, cols):
+        pl.semaphore_signal(barrier, 1, device_id={"cont": lax.rem(j + k, cols)})
 
     def first_up_copy(h):
         part = pl.ds(NBLK + h * HALF, HALF)
@@ -384,6 +384,26 @@
             hop_copy(0).wait_recv()
             hop_copy(1).start()
 
+    def end_earlier_sends():
+        for s in range(STEPS):
+            if 0 < s < STEPS - 1:
+                up_copy(s).wait_send()
+            if s < 2 * CHUNKS:
+                low_copy(s).wait_send()
+            for k in range(1, cols):
+                con_copy(s, k).wait_send()
+        for n in range(2):
+            hop_copy(n).wait_send()
+        for h in range(2):
+            first_up_copy(h).wait_send()
+        for k in range(1, cols):
+            flag_copy(k).wait_send()
+        for a in range(2 * CHUNKS):
+            for k in range(1, rows):
+                sub_copy(a, k).wait_send()
+            for k in range(1, cols):
+                cont_copy(a, k).wait_send()
+
     scales = []
     for c in range(CHUNKS):
         new_norm, cross, curv = end_sum(CHUNKS + c, 3)
@@ -426,6 +446,7 @@
             up_copy(2 * CHUNKS).wait_recv()
             hop_copy(2).wait_recv()
         else:
+            end_earlier_sends()
             last_up_copy(0).wait_recv()
             last_up_copy(1).wait_recv()
 
@@ -436,25 +457,9 @@
             return 0
         lax.fori_loop(0, NBLK, glue_res, 0)
 
-    for s in range(STEPS):
-        if 0 < s < STEPS - 1:
-            up_copy(s).wait_send()
-        if s < 2 * CHUNKS:
-            low_copy(s).wait_send()
-        for k in range(1, cols):
-            con_copy(s, k).wait_send()
-    for n in range(3):
-        hop_copy(n).wait_send()
-    for h in range(2):
-        first_up_copy(h).wait_send()
-        last_up_copy(h).wait_send()
-    for k in range(1, cols):
-        flag_copy(k).wait_send()
-    for a in range(2 * CHUNKS):
-        for k in range(1, rows):
-            sub_copy(a, k).wait_send()
-        for k in range(1, cols):
-            cont_copy(a, k).wait_send()
+    last_up_copy(0).wait_send()
+    last_up_copy(1).wait_send()
+    hop_copy(2).wait_send()
 
 
 def hand_on(*refs):

time: 82.3 us -> 82.1 us (level)
  no operation moved by 1% of the time
where the time goes in v6:
time: 82.1 us; the launch traced here: 81.8 us
  Pallas kernels  81.2 us (99%)
    pallas_call x1, Pallas kernels, per_device(): pl.pallas_call(lambda *refs: kernel(rows, cols, *refs), out_shape=[pltpu....  79.1 us
    pallas_call x1, Pallas kernels, per_device(): pl.pallas_call(hand_on, out_shape=[jax.ShapeDtypeStruct((FACE, LOADS), F3...  2.04 us

profile of v6, /device:TPU:1, one launch (start us, length us, event | category | flops | bytes accessed | tf_op | source)
XLA Modules:
  0.0 81.8 jit_solution(2660369281408246472)
XLA Ops:
  0.6 79.1 %shard_map.84 = (f32[512,512]{1,0:T(8,128)S(1)}, f32[512,512]{1,0:T(8,128)S(1)}, f32[512,512]{1,0:T(8,128)S(1)}, f32[512,512]{1,0:T(8,128)S(1)}) custom-call(f32[1536,1536]{1,0:T(8,128)} %bitcast.9, f32[1536,512]{1,0:T(8,128)} %bitcast.10, s32[1,8]{1,0:T(1,128)} %bitcast.16, s32[1,8]{1,0:T(1,128)} %bitcast.17, s32[1,512]{1,0:T(1,128)} %bitcast.15), custom_call_target="tpu_custom_call" | custom-call | flops 21743271936 | bytes 16777216 | tf_op jit(solution)/shard_map/pallas_call | solution.py:480
  79.8 2.0 %shard_map.85 = (f32[512,512]{1,0:T(8,128)}, f32[512,512]{1,0:T(8,128)}, f32[512,512]{1,0:T(8,128)}, f32[512,512]{1,0:T(8,128)}) custom-call(f32[512,512]{1,0:T(8,128)S(1)} %get-tuple-element.12.refs_0_, f32[512,512]{1,0:T(8,128)S(1)} %get-tuple-element.13.refs_1_, f32[512,512]{1,0:T(8,128)S(1)} %get-tuple-element.14.refs_2_, ...), custom_call_target="tpu_custom_call" | custom-call | tf_op jit(solution)/shard_map/pallas_call | solution.py:532
